TPU v7x, 32 devices: a whole 2x2x4 slice. The times are simulated.
32 devices in a mesh: dp: 8 (over z, x), tensor: 4 (over y, core).
Axes of the slice: x: 2, y: 2, z: 4, core: 2. Of those that a mesh axis runs over, the one named last changes fastest.
Arguments:
- layer_input: bfloat16 [4096, 768], P('dp', 'tensor'), may hold values from -6 to 6
- segment_ids: int32 [8, 512], P('dp'), may hold values from 0 to 15, never falling along the last dimension, each value on 1 to 256 neighbouring positions
- triple_weight: bfloat16 [768, 3, 768], P(None, None, 'tensor'), may hold values from -0.21875 to 0.21875
- query_value_bias: float32 [2, 768], P(None, 'tensor'), may hold values from -3 to 3
- output_weight: bfloat16 [768, 768], P('tensor'), may hold values from -0.875 to 0.875
- output_bias: float32 [768], P('tensor'), may hold values from -3 to 3
- norm_gain: float32 [768], P('tensor'), may hold values from 0.5 to 1.5
- norm_shift: float32 [768], P('tensor'), may hold values from -3 to 3
- expand_weight: bfloat16 [768, 3072], P(None, 'tensor'), may hold values from -0.21875 to 0.21875
- expand_bias: float32 [3072], P('tensor'), may hold values from -3 to 3
- reduce_weight: bfloat16 [3072, 768], P('tensor'), may hold values from -0.109375 to 0.109375
- reduce_bias: float32 [768], P('tensor'), may hold values from -3 to 3
- final_gain: float32 [768], P('tensor'), may hold values from 0.5 to 1.5
- final_shift: float32 [768], P('tensor'), may hold values from -3 to 3
- cotangent: bfloat16 [4096, 768], P('dp', 'tensor'), may hold values from -6 to 6
Outputs:
- layer_output: bfloat16 [4096, 768], P('dp', 'tensor')
- input_grad: float32 [4096, 768], P('dp', 'tensor')
- triple_grad: float32 [768, 3, 768], P(None, None, 'tensor')
- query_value_grad: float32 [2, 768], P(None, 'tensor')
- output_weight_grad: float32 [768, 768], P('tensor')
- output_bias_grad: float32 [768], P('tensor')
- norm_gain_grad: float32 [768], P('tensor')
- norm_shift_grad: float32 [768], P('tensor')
- expand_weight_grad: float32 [768, 3072], P(None, 'tensor')
- expand_bias_grad: float32 [3072], P('tensor')
- reduce_weight_grad: float32 [3072, 768], P('tensor')
- reduce_bias_grad: float32 [768], P('tensor')
- final_gain_grad: float32 [768], P('tensor')
- final_shift_grad: float32 [768], P('tensor')
Inputs may be any that keep to these rules, and one draw needn't show every extreme that they name: `segment_ids`: segment numbers never fall along a sequence; each document holds 1 to 256 tokens.
All inputs are finite; a program needn't handle non-finite values.
Results may differ from a plain program's by a relative error of at most 0.012.
The roundings to bfloat16 on the way count: a program that leaves them out, or rounds other values in their place, can miss the bound.
Values may be sent and summed in bfloat16 or wider, within the bound.
A program may use at most 64 MiB of HBM per device.

v0:
```python
import jax
import jax.numpy as jnp
from jax import lax
from jax.sharding import PartitionSpec as P

D = 768
HD = 64
EPS = 1e-06


def gelu_value(pre_act):
    return 0.5 * pre_act * (1.0 + lax.erf(pre_act * 0.7071067811865476))


def gelu_slope(pre_act):
    return (
        0.5 * (1.0 + lax.erf(pre_act * 0.7071067811865476))
        + pre_act * jnp.exp(-0.5 * pre_act * pre_act) * 0.3989422804014327
    )


def norm_forward(hidden, gain, shift):
    row_mean = jnp.mean(hidden, axis=-1, keepdims=True)
    centred = hidden - row_mean
    inverse = lax.rsqrt(jnp.mean(centred * centred, axis=-1, keepdims=True) + EPS)
    normed = centred * inverse
    return (normed * gain + shift, normed, inverse)


def norm_backward(upstream, normed, inverse, gain):
    scaled = upstream * gain
    first_mean = jnp.mean(scaled, axis=-1, keepdims=True)
    second_mean = jnp.mean(scaled * normed, axis=-1, keepdims=True)
    return inverse * (scaled - first_mean - normed * second_mean)


def sum_rows(partial):
    return lax.psum_scatter(
        partial.astype(jnp.bfloat16), "tensor", scatter_dimension=0, tiled=True
    ).astype(jnp.float32)


def all_rows(piece):
    return lax.all_gather(piece, "tensor", axis=0, tiled=True)


def column_sum(rows):
    return jnp.sum(rows, axis=0)


def tall_dot(left, right):
    return lax.dot_general(
        left, right, (((0,), (0,)), ((), ())), preferred_element_type=jnp.float32
    )


def wide_dot(left, right):
    return lax.dot_general(
        left, right, (((1,), (1,)), ((), ())), preferred_element_type=jnp.float32
    )


def masked_scores(query_part, key_part, segment_row, head_scale):
    scores = (
        jnp.einsum("qhd,khd->hqk", query_part, key_part, preferred_element_type=jnp.float32)
        * head_scale
    )
    allowed = segment_row[:, None] == segment_row[None, :]
    return jnp.where(allowed[None], scores, -jnp.inf)


def per_device(
    layer_input,
    segment_ids,
    triple_weight,
    query_value_bias,
    output_weight,
    output_bias,
    norm_gain,
    norm_shift,
    expand_weight,
    expand_bias,
    reduce_weight,
    reduce_bias,
    final_gain,
    final_shift,
    cotangent,
):
    seq_len = segment_ids.shape[1]
    tok_count = segment_ids.shape[0] * seq_len
    local_width = triple_weight.shape[2]
    local_heads = local_width // HD
    head_scale = HD ** (-0.5)
    groups = lax.axis_size("tensor")
    rank = lax.axis_index("tensor")
    block = tok_count // groups
    both = lax.all_gather(
        jnp.concatenate([layer_input, cotangent], axis=0), "tensor", axis=1, tiled=True
    )
    gathered = both[:tok_count]
    own_input = lax.dynamic_slice_in_dim(both, rank * block, block, 0).astype(jnp.float32)
    upstream = lax.dynamic_slice_in_dim(both, tok_count + rank * block, block, 0).astype(
        jnp.float32
    )
    vectors = lax.all_gather(
        jnp.stack([output_bias, norm_gain, norm_shift, reduce_bias, final_gain, final_shift]),
        "tensor",
        axis=1,
        tiled=True,
    )
    output_bias, norm_gain, norm_shift, reduce_bias, final_gain, final_shift = [
        vectors[i] for i in range(6)
    ]
    projected = jnp.einsum(
        "td,dcf->tcf", gathered, triple_weight, preferred_element_type=jnp.float32
    )
    query_half = (
        (projected[:, 0] + query_value_bias[0])
        .astype(jnp.bfloat16)
        .reshape(seq_len, local_heads, HD)
    )
    key_half = projected[:, 1].astype(jnp.bfloat16).reshape(seq_len, local_heads, HD)
    value_half = (
        (projected[:, 2] + query_value_bias[1])
        .astype(jnp.bfloat16)
        .reshape(seq_len, local_heads, HD)
    )
    scores = masked_scores(query_half, key_half, segment_ids[0], head_scale)
    top = jnp.max(scores, axis=-1, keepdims=True)
    log_total = top + jnp.log(jnp.sum(jnp.exp(scores - top), axis=-1, keepdims=True))
    probs_half = jnp.exp(scores - log_total).astype(jnp.bfloat16)
    context = jnp.einsum(
        "hqk,khd->qhd", probs_half, value_half, preferred_element_type=jnp.float32
    ).astype(jnp.bfloat16)
    context_flat = context.reshape(tok_count, local_width)
    first_sum = (
        own_input
        + sum_rows(jnp.dot(context_flat, output_weight, preferred_element_type=jnp.float32))
        + output_bias
    )
    attended, normed_one, inv_one = norm_forward(first_sum, norm_gain, norm_shift)
    attended_half = all_rows(attended.astype(jnp.bfloat16))
    pre_act = (
        jnp.dot(attended_half, expand_weight, preferred_element_type=jnp.float32) + expand_bias
    )
    activated = gelu_value(pre_act).astype(jnp.bfloat16)
    second_sum = (
        attended
        + sum_rows(jnp.dot(activated, reduce_weight, preferred_element_type=jnp.float32))
        + reduce_bias
    )
    out_f, normed_two, inv_two = norm_forward(second_sum, final_gain, final_shift)
    layer_output = lax.all_to_all(
        out_f.astype(jnp.bfloat16), "tensor", split_axis=1, concat_axis=0, tiled=True
    )
    final_gain_grad = column_sum(upstream * normed_two)
    final_shift_grad = column_sum(upstream)
    second_grad = norm_backward(upstream, normed_two, inv_two, final_gain)
    second_half = all_rows(second_grad.astype(jnp.bfloat16))
    reduce_weight_grad = tall_dot(activated, second_half)
    reduce_bias_grad = column_sum(second_grad)
    act_grad = wide_dot(second_half, reduce_weight) * gelu_slope(pre_act)
    act_half = act_grad.astype(jnp.bfloat16)
    expand_weight_grad = tall_dot(attended_half, act_half)
    expand_bias_grad = column_sum(act_grad)
    feed_sum = lax.psum(
        jnp.concatenate([reduce_weight_grad, expand_weight_grad], axis=0).astype(jnp.bfloat16), "dp"
    )
    split = reduce_weight_grad.shape[0]
    attended_grad = second_grad + sum_rows(wide_dot(act_half, expand_weight))
    norm_gain_grad = column_sum(attended_grad * normed_one)
    norm_shift_grad = column_sum(attended_grad)
    first_grad = norm_backward(attended_grad, normed_one, inv_one, norm_gain)
    first_half = all_rows(first_grad.astype(jnp.bfloat16))
    output_weight_grad = tall_dot(context_flat, first_half)
    output_bias_grad = column_sum(first_grad)
    grad_part = (
        wide_dot(first_half, output_weight).astype(jnp.bfloat16).reshape(seq_len, local_heads, HD)
    )
    scores = masked_scores(query_half, key_half, segment_ids[0], head_scale)
    probs = jnp.exp(scores - log_total)
    probs_half = probs.astype(jnp.bfloat16)
    value_grad = jnp.einsum(
        "hqk,qhd->khd", probs_half, grad_part, preferred_element_type=jnp.float32
    ).reshape(tok_count, local_width)
    prob_grad = jnp.einsum(
        "qhd,khd->hqk", grad_part, value_half, preferred_element_type=jnp.float32
    )
    delta = jnp.einsum("qhd,qhd->hq", grad_part.astype(jnp.float32), context.astype(jnp.float32))
    score_grad = (probs * (prob_grad - delta[:, :, None]) * head_scale).astype(jnp.bfloat16)
    query_grad = jnp.einsum(
        "hqk,khd->qhd", score_grad, key_half, preferred_element_type=jnp.float32
    ).reshape(tok_count, local_width)
    key_grad = jnp.einsum(
        "hqk,qhd->khd", score_grad, query_half, preferred_element_type=jnp.float32
    ).reshape(tok_count, local_width)
    triple_half = jnp.stack([query_grad, key_grad, value_grad], axis=1).astype(jnp.bfloat16)
    triple_grad = jnp.einsum(
        "td,tcf->dcf", gathered, triple_half, preferred_element_type=jnp.float32
    )
    input_terms = jnp.einsum(
        "tcf,dcf->td", triple_half, triple_weight, preferred_element_type=jnp.float32
    )
    smalls = jnp.stack(
        [
            output_bias_grad,
            norm_gain_grad,
            norm_shift_grad,
            reduce_bias_grad,
            final_gain_grad,
            final_shift_grad,
        ]
    )
    own_rows = lax.dynamic_slice_in_dim(input_terms, rank * block, block, 0) + first_grad
    input_terms = lax.dynamic_update_slice_in_dim(input_terms, own_rows, rank * block, 0)
    shares = lax.psum_scatter(
        jnp.concatenate([input_terms, smalls, jnp.zeros((10, D), jnp.float32)], axis=0).astype(
            jnp.bfloat16
        ),
        "tensor",
        scatter_dimension=1,
        tiled=True,
    ).astype(jnp.float32)
    input_grad = shares[:tok_count]
    pieces = [
        triple_grad,
        output_weight_grad,
        expand_bias_grad,
        jnp.sum(query_grad, axis=0),
        jnp.sum(value_grad, axis=0),
        shares[tok_count : tok_count + 6],
    ]
    packed = jnp.concatenate([p.reshape(-1, local_width) for p in pieces], axis=0)
    packed, feed_sum = lax.optimization_barrier((packed.astype(jnp.bfloat16), feed_sum))
    packed = lax.psum(packed, "dp").astype(jnp.float32)
    reduce_weight_grad = feed_sum[:split].astype(jnp.float32)
    expand_weight_grad = feed_sum[split:].astype(jnp.float32)
    outs, at = ([], 0)
    for p in pieces:
        count = p.size // local_width
        outs.append(packed[at : at + count].reshape(p.shape))
        at += count
    triple_grad, output_weight_grad, expand_bias_grad, query_sum, value_sum, small_sums = outs
    return (
        layer_output,
        input_grad,
        triple_grad,
        jnp.stack([query_sum, value_sum]),
        output_weight_grad,
        small_sums[0],
        small_sums[1],
        small_sums[2],
        expand_weight_grad,
        expand_bias_grad,
        reduce_weight_grad,
        small_sums[3],
        small_sums[4],
        small_sums[5],
    )


def solution(mesh):
    in_specs = (
        P("dp", "tensor"),
        P("dp", None),
        P(None, None, "tensor"),
        P(None, "tensor"),
        P("tensor", None),
        P("tensor"),
        P("tensor"),
        P("tensor"),
        P(None, "tensor"),
        P("tensor"),
        P("tensor", None),
        P("tensor"),
        P("tensor"),
        P("tensor"),
        P("dp", "tensor"),
    )
    out_specs = (
        P("dp", "tensor"),
        P("dp", "tensor"),
        P(None, None, "tensor"),
        P(None, "tensor"),
        P("tensor", None),
        P("tensor"),
        P("tensor"),
        P("tensor"),
        P(None, "tensor"),
        P("tensor"),
        P("tensor", None),
        P("tensor"),
        P("tensor"),
        P("tensor"),
    )
    return jax.shard_map(
        per_device, mesh=mesh, in_specs=in_specs, out_specs=out_specs, check_vma=False
    )
```

profile of v0, /device:TPU:0, one launch (start us, length us, event | category | flops | bytes accessed | tf_op | source)
XLA Modules:
  0.0 413.7 jit_solution(5651966376495020116)
XLA Ops:
  7.2 1.9 pad_maximum_fusion.2
  11.1 21.4 %all-gather.3.cloned.1.call-done = bf16[1024,768]{0,1:T(8,128)(2,1)} async-done(((bf16[1024,192]{0,1:T(8,128)(2,1)}), bf16[1024,768]{0,1:T(8,128)(2,1)}) %all-gather.3.cloned.1.call-update) | async-done | bytes 1572880 | tf_op jit(solution)/shard_map/all_gather | solution.py:97
  32.6 2.0 fusion.7
  39.7 5.2 %all-gather = f32[4,192,6]{1,2,0:T(8,128)S(1)} all-gather(f32[1,192,6]{1,2,0:T(8,128)S(1)} %bitcast.109), channel_id=1, replica_groups=mesh['dp'=8,'tensor'=4] {'tensor'}, dimensions={0}, use_global_device_ids=true | all-gather | bytes 23040 | tf_op jit(solution)/shard_map/all_gather | solution.py:105
  46.4 16.6 %reduce-scatter.7.cloned.1.call-done = bf16[128,768]{1,0:T(8,128)(2,1)} async-done(((bf16[512,768]{1,0:T(8,128)(2,1)}), bf16[128,768]{1,0:T(8,128)(2,1)}) %reduce-scatter.7.cloned.1.call-update) | async-done | bytes 196624 | tf_op jit(solution)/shard_map/reduce_scatter | solution.py:38
  66.2 8.2 %all_gather.17 = bf16[512,768]{1,0:T(8,128)(2,1)S(1)} all-gather(bf16[128,768]{1,0:T(8,128)(2,1)S(1)} %fusion.21), channel_id=1, replica_groups=mesh['dp'=8,'tensor'=4] {'tensor'}, dimensions={0}, use_global_device_ids=true | all-gather | bytes 983040 | tf_op jit(solution)/shard_map/all_gather | solution.py:44
  74.5 2.0 multiply_convert_fusion.1
  79.3 23.6 %reduce-scatter.9.cloned.1.call-done = bf16[128,768]{1,0:T(8,128)(2,1)} async-done(((bf16[512,768]{1,0:T(8,128)(2,1)}), bf16[128,768]{1,0:T(8,128)(2,1)}) %reduce-scatter.9.cloned.1.call-update) | async-done | bytes 196624 | tf_op jit(solution)/shard_map/reduce_scatter | solution.py:38
  105.5 8.2 %all_gather.18 = bf16[512,768]{1,0:T(8,128)(2,1)S(1)} all-gather(bf16[128,768]{1,0:T(8,128)(2,1)S(1)} %get-tuple-element.94), channel_id=1, replica_groups=mesh['dp'=8,'tensor'=4] {'tensor'}, dimensions={0}, use_global_device_ids=true | all-gather | bytes 983040 | tf_op jit(solution)/shard_map/all_gather | solution.py:44
  118.0 23.7 %reduce-scatter.11.cloned.1.call-done = bf16[128,768]{1,0:T(8,128)(2,1)} async-done(((bf16[512,768]{1,0:T(8,128)(2,1)}), bf16[128,768]{1,0:T(8,128)(2,1)}) %reduce-scatter.11.cloned.1.call-update) | async-done | bytes 196624 | tf_op jit(solution)/shard_map/reduce_scatter | solution.py:38
  144.3 8.5 %all_gather.19 = bf16[512,768]{1,0:T(8,128)(2,1)S(1)} all-gather(bf16[128,768]{1,0:T(8,128)(2,1)S(1)} %convert_element_type.106), channel_id=1, replica_groups=mesh['dp'=8,'tensor'=4] {'tensor'}, dimensions={0}, use_global_device_ids=true | all-gather | bytes 983040 | tf_op jit(solution)/shard_map/all_gather | solution.py:44
  159.4 3.1 concatenate.16
  163.9 2.3 convolution_convert_fusion.1
  172.2 2.5 copy.72
  174.8 2.2 reshape.172
  178.9 10.0 %reduce-scatter.13.cloned.1.call-done = bf16[192,528]{1,0:T(8,128)(2,1)} async-done(((bf16[768,528]{1,0:T(8,128)(2,1)}), bf16[192,528]{1,0:T(8,128)(2,1)}) %reduce-scatter.13.cloned.1.call-update) | async-done | bytes 202768
  189.8 6.7 %concatenate.17 = bf16[3084,192]{1,0:T(8,128)(2,1)} concatenate(bf16[2304,192]{1,0:T(8,128)(2,1)S(1)} %copy-done.5, bf16[768,192]{1,0:T(8,128)(2,1)S(1)} %reshape.173, bf16[4,192]{1,0:T(4,128)(2,1)S(1)} %reshape.174, bf16[1,192]{1,0:T(2,128)(2,1)S(1)} %reshape.175, bf16[1,192]{1,0:T(2,128)(2,1)S(1)} %reshape.176, bf16[6,192]{1,0:T(8,128)(2,1)S(1)} %copy.93), dimensions={0} | concatenate | bytes 2368512 | tf_op jit(solution)/shard_map/concatenate | solution.py:233
  196.5 105.1 %all-reduce.3.cloned.1.call-done = bf16[1536,768]{1,0:T(8,128)(2,1)} async-done(((bf16[1536,768]{1,0:T(8,128)(2,1)}), bf16[1536,768]{1,0:T(8,128)(2,1)}) %all-reduce.3.cloned.1.call-update) | async-done | bytes 2359312 | tf_op jit(solution)/shard_map/psum | solution.py:166
  301.7 1.9 copy.65
  303.6 8.7 %all_to_all.19 = bf16[128,4,192]{0,2,1:T(8,128)(2,1)S(1)} all-to-all(bf16[128,4,192]{0,2,1:T(8,128)(2,1)} %bitcast.101), channel_id=1, replica_groups=mesh['dp'=8,'tensor'=4] {'tensor'}, dimensions={1} | all-to-all | bytes 393216 | tf_op jit(solution)/shard_map/all_to_all | solution.py:153
  318.1 2.5 slice_convert_fusion
  320.7 74.8 %all-reduce.5.cloned.1.call-done = bf16[3084,192]{1,0:T(8,128)(2,1)} async-done(((bf16[3084,192]{1,0:T(8,128)(2,1)}), bf16[3084,192]{1,0:T(8,128)(2,1)}) %all-reduce.5.cloned.1.call-update) | async-done | bytes 1184272 | tf_op jit(solution)/shard_map/psum | solution.py:235
  396.9 2.6 reshape.177
  399.5 4.3 %copy.74 = f32[768,3,192]{0,2,1:T(8,128)} copy(f32[768,3,192]{2,1,0:T(4,128)} %reshape.177) | data formatting | bytes 3538944
  (160 shorter events, 50.9 us)
Async XLA Ops:
  7.2 67.3 %copy-start = (bf16[768,768]{1,0:T(8,128)(2,1)S(1)}, bf16[768,768]{1,0:T(8,128)(2,1)}, u32[]{:S(2)}) copy-start(bf16[768,768]{1,0:T(8,128)(2,1)} %param.23) | copy-start | bytes 3538948
  7.2 25.4 %all-gather.3.cloned.1.call-start = ((), (), s32[]{:S(2)}) async-start(), calls=%async_computation.5 | async-start | bytes 1966080 | tf_op jit(solution)/shard_map/all_gather | solution.py:97
  9.2 53.8 %reduce-scatter.7.cloned.1.call-start = ((), (), s32[]{:S(2)}) async-start(), calls=%async_computation.6 | async-start | bytes 983040 | tf_op jit(solution)/shard_map/reduce_scatter | solution.py:38
  38.1 115.1 %copy-start.8 = (bf16[3,64,512]{2,1,0:T(8,128)(2,1)}, bf16[3,64,512]{2,1,0:T(8,128)(2,1)S(1)}, u32[]{:S(2)}) copy-start(bf16[3,64,512]{2,1,0:T(8,128)(2,1)S(1)} %convolution_convert_fusion.7) | copy-start | bytes 589828
  39.5 63.4 %reduce-scatter.9.cloned.1.call-start = ((), (), s32[]{:S(2)}) async-start(), calls=%async_computation.7 | async-start | bytes 983040 | tf_op jit(solution)/shard_map/reduce_scatter | solution.py:38
  46.2 28.2 %copy-start.29 = (f32[768]{0:T(1024)S(1)}, f32[768]{0:T(1024)}, u32[]{:S(2)}) copy-start(f32[768]{0:T(1024)} %param.24) | copy-start | bytes 9220
  74.5 2.0 copy-start.13
  74.5 3.0 copy-start.27
  77.4 25.5 %copy-start.3 = (bf16[128,768]{1,0:T(8,128)(2,1)S(1)}, bf16[128,768]{1,0:T(8,128)(2,1)}, u32[]{:S(2)}) copy-start(bf16[128,768]{1,0:T(8,128)(2,1)} %reduce-scatter.7.cloned.1.call-done) | copy-start | bytes 589828
  79.1 62.7 %reduce-scatter.11.cloned.1.call-start = ((), (), s32[]{:S(2)}) async-start(), calls=%async_computation.8 | async-start | bytes 983040 | tf_op jit(solution)/shard_map/reduce_scatter | solution.py:38
  104.3 9.4 %copy-start.28 = (bf16[768,768]{1,0:T(8,128)(2,1)S(1)}, bf16[768,768]{1,0:T(8,128)(2,1)}, u32[]{:S(2)}) copy-start(bf16[768,768]{1,0:T(8,128)(2,1)} %param.25) | copy-start | bytes 3538948
  104.3 9.4 %copy-start.33 = (f32[512,768]{1,0:T(8,128)S(1)}, f32[512,768]{1,0:T(8,128)}, u32[]{:S(2)}) copy-start(f32[512,768]{1,0:T(8,128)} %get-tuple-element.117) | copy-start | bytes 4718596
  118.0 70.9 %reduce-scatter.13.cloned.1.call-start = ((), (), s32[]{:S(2)}) async-start(), calls=%async_computation.11 | async-start | bytes 1228800
  143.1 10.3 %copy-start.17 = (f32[512,1,192]{0,2,1:T(8,128)S(1)}, f32[512,1,192]{0,2,1:T(8,128)}, u32[]{:S(2)}) copy-start(f32[512,1,192]{0,2,1:T(8,128)} %copy-done.16) | copy-start | bytes 1179652
  144.3 9.1 %copy-start.2 = (f32[3,512,512]{1,2,0:T(8,128)S(1)}, f32[3,512,512]{1,2,0:T(8,128)}, u32[]{:S(2)}) copy-start(f32[3,512,512]{1,2,0:T(8,128)} %copy-done.1) | copy-start | bytes 9437188
  155.2 2.3 copy-start.11
  163.8 2.4 copy-start.14
  163.9 2.4 copy-start.32
  163.9 137.8 %all-reduce.3.cloned.1.call-start = ((), (), s32[]{:S(2)}) async-start(), calls=%async_computation.9 | async-start | bytes 4718592 | tf_op jit(solution)/shard_map/psum | solution.py:166
  168.6 2.0 copy-start.6
  168.6 226.9 %all-reduce.5.cloned.1.call-start = ((), (), s32[]{:S(2)}) async-start(), calls=%async_computation.10 | async-start | bytes 3162112 | tf_op jit(solution)/shard_map/psum | solution.py:235
  177.0 12.8 %copy-start.5 = (bf16[2304,192]{1,0:T(8,128)(2,1)S(1)}, bf16[2304,192]{1,0:T(8,128)(2,1)}, u32[]{:S(2)}) copy-start(bf16[2304,192]{1,0:T(8,128)(2,1)} %reshape.172) | copy-start | bytes 2654212
  301.7 16.5 %copy-start.7 = (bf16[1536,768]{1,0:T(8,128)(2,1)S(1)}, bf16[1536,768]{1,0:T(8,128)(2,1)}, u32[]{:S(2)}) copy-start(bf16[1536,768]{1,0:T(8,128)(2,1)} %all-reduce.3.cloned.1.call-done) | copy-start | bytes 7077892
  399.5 4.3 %copy-start.4 = (bf16[3084,192]{1,0:T(8,128)(2,1)S(1)}, bf16[3084,192]{1,0:T(8,128)(2,1)}, u32[]{:S(2)}) copy-start(bf16[3084,192]{1,0:T(8,128)(2,1)} %all-reduce.5.cloned.1.call-done) | copy-start | bytes 3552772
  (17 other events, 23.2 us)
Sparse Core Ops, SparseCore 0:
  10.2 22.3 all-gather.2
  39.7 23.2 reduce-scatter.6
  79.2 23.6 reduce-scatter.8
  118.1 23.6 reduce-scatter.10
  164.0 24.8 reduce-scatter.12
  192.9 108.7 all-reduce.2
  306.2 89.2 all-reduce.4
where the time goes:
time: 415 us; the launch traced here: 414 us
  waiting for transfers between devices  275 us (66%)
  local copies, waits for them, and re-layouts  41.6 us (10%)
  blocking collectives  38.8 us (9%)
  matrix products  22.5 us (5%)
  other arithmetic  20.5 us (5%)
  between operations  14.7 us (4%)
    psum x1, waiting for transfers between devices, per_device(): lax.psum(jnp.concatenate([reduce_weight_grad, expand_weight_grad], axis=0...  105 us
    psum x1, waiting for transfers between devices, per_device(): packed = lax.psum(packed, 'dp').astype(jnp.float32)  74.8 us
    reduce_scatter x3, waiting for transfers between devices, sum_rows(): lax.psum_scatter(partial.astype(jnp.bfloat16), 'tensor', scatter_dimensio...  63.9 us
    all_gather x3, blocking collectives, all_rows(): return lax.all_gather(piece, 'tensor', axis=0, tiled=True)  24.9 us
    all_gather x1, waiting for transfers between devices, per_device(): lax.all_gather(jnp.concatenate([layer_input, cotangent], axis=0), 'tensor...  21.4 us
    unnamed x76, local copies, waits for them, and re-layouts  13.2 us
    unnamed x8, waiting for transfers between devices  10.1 us
    all_to_all x1, blocking collectives, per_device(): lax.all_to_all(out_f.astype(jnp.bfloat16), 'tensor', split_axis=1, concat...  8.67 us
  transfers between devices with their start and end apart: 7, of which 7 were waited for; matrix products, arithmetic and copies ran while one was open for 9% of the time, Pallas kernels for 0%

commit v1 on v0

--- a/solution.py
+++ b/solution.py
@@ -232,7 +232,12 @@
     ]
     packed = jnp.concatenate([p.reshape(-1, local_width) for p in pieces], axis=0)
     packed, feed_sum = lax.optimization_barrier((packed.astype(jnp.bfloat16), feed_sum))
-    packed = lax.psum(packed, "dp").astype(jnp.float32)
+
+    def cut_frame(a0, axis_key="dp"):
+        arr_out = lax.all_gather(a0, axis_key)
+        return jnp.sum(arr_out, axis=0)
+
+    packed = cut_frame(packed).astype(jnp.float32)
     reduce_weight_grad = feed_sum[:split].astype(jnp.float32)
     expand_weight_grad = feed_sum[split:].astype(jnp.float32)
     outs, at = ([], 0)

time: 415 us -> 474 us (1.14)
  waiting for transfers between devices: 275 us -> 342 us
  local copies, waits for them, and re-layouts: 41.6 us -> 30.5 us
  other arithmetic: 20.5 us -> 25.9 us
    all_gather x0 -> x1, waiting for transfers between devices: none -> 131 us  [cut_frame(): arr_out = lax.all_gather(a0, axis_key)]
    psum x1 -> x0, waiting for transfers between devices: 74.8 us -> none  [per_device(): packed = lax.psum(packed, 'dp').astype(jnp.float32)]
    psum x1, waiting for transfers between devices: 105 us -> 111 us  [per_device(): lax.psum(jnp.concatenate([reduce_weight_grad, expand_weight_grad], axis=0...]
    concatenate x1, local copies, waits for them, and re-layouts: 6.74 us -> 0.55 us  [per_device(): jnp.concatenate([p.reshape(-1, local_width) for p in pieces], axis=0)]
    reduce_sum x0 -> x1, other arithmetic: none -> 5.83 us  [cut_frame(): return jnp.sum(arr_out, axis=0)]
    unnamed x76 -> x84, local copies, waits for them, and re-layouts: 13.2 us -> 13 us
  transfers between devices with their start and end apart: 7 -> 7, of which waited for: 7 -> 7; matrix products, arithmetic and copies ran while one was open for 9% -> 4% of each run, Pallas kernels for 0% -> 0%
where the time goes in v1:
time: 474 us; the launch traced here: 473 us
  waiting for transfers between devices  342 us (72%)
  blocking collectives  38.1 us (8%)
  local copies, waits for them, and re-layouts  30.5 us (6%)
  other arithmetic  25.9 us (5%)
  matrix products  21.9 us (5%)
  between operations  14.8 us (3%)
    all_gather x1, waiting for transfers between devices, cut_frame(): arr_out = lax.all_gather(a0, axis_key)  131 us
    psum x1, waiting for transfers between devices, per_device(): lax.psum(jnp.concatenate([reduce_weight_grad, expand_weight_grad], axis=0...  111 us
    reduce_scatter x3, waiting for transfers between devices, sum_rows(): lax.psum_scatter(partial.astype(jnp.bfloat16), 'tensor', scatter_dimensio...  63.9 us
    all_gather x3, blocking collectives, all_rows(): return lax.all_gather(piece, 'tensor', axis=0, tiled=True)  24.9 us
    all_gather x1, waiting for transfers between devices, per_device(): lax.all_gather(jnp.concatenate([layer_input, cotangent], axis=0), 'tensor...  21.4 us
    unnamed x8, waiting for transfers between devices  14.4 us
    unnamed x84, local copies, waits for them, and re-layouts  13 us
  transfers between devices with their start and end apart: 7, of which 7 were waited for; matrix products, arithmetic and copies ran while one was open for 4% of the time, Pallas kernels for 0%

profile of v1, /device:TPU:0, one launch (start us, length us, event | category | flops | bytes accessed | tf_op | source)
XLA Modules:
  0.0 473.2 jit_solution(12467113648468604102)
XLA Ops:
  7.2 1.9 pad_maximum_fusion.2
  11.1 21.4 %all-gather.6.cloned.1.call-done = bf16[1024,768]{0,1:T(8,128)(2,1)} async-done(((bf16[1024,192]{0,1:T(8,128)(2,1)}), bf16[1024,768]{0,1:T(8,128)(2,1)}) %all-gather.6.cloned.1.call-update) | async-done | bytes 1572880 | tf_op jit(solution)/shard_map/all_gather | solution.py:97
  32.6 2.0 fusion.7
  39.7 5.2 %all-gather.1 = f32[4,192,6]{1,2,0:T(8,128)S(1)} all-gather(f32[1,192,6]{1,2,0:T(8,128)S(1)} %bitcast.105), channel_id=1, replica_groups=mesh['dp'=8,'tensor'=4] {'tensor'}, dimensions={0}, use_global_device_ids=true | all-gather | bytes 23040 | tf_op jit(solution)/shard_map/all_gather | solution.py:105
  46.4 16.6 %reduce-scatter.7.cloned.1.call-done = bf16[128,768]{1,0:T(8,128)(2,1)} async-done(((bf16[512,768]{1,0:T(8,128)(2,1)}), bf16[128,768]{1,0:T(8,128)(2,1)}) %reduce-scatter.7.cloned.1.call-update) | async-done | bytes 196624 | tf_op jit(solution)/shard_map/reduce_scatter | solution.py:38
  66.2 8.2 %all_gather.23 = bf16[512,768]{1,0:T(8,128)(2,1)S(1)} all-gather(bf16[128,768]{1,0:T(8,128)(2,1)S(1)} %fusion.21), channel_id=1, replica_groups=mesh['dp'=8,'tensor'=4] {'tensor'}, dimensions={0}, use_global_device_ids=true | all-gather | bytes 983040 | tf_op jit(solution)/shard_map/all_gather | solution.py:44
  74.5 2.0 multiply_convert_fusion.1
  79.3 23.6 %reduce-scatter.9.cloned.1.call-done = bf16[128,768]{1,0:T(8,128)(2,1)} async-done(((bf16[512,768]{1,0:T(8,128)(2,1)}), bf16[128,768]{1,0:T(8,128)(2,1)}) %reduce-scatter.9.cloned.1.call-update) | async-done | bytes 196624 | tf_op jit(solution)/shard_map/reduce_scatter | solution.py:38
  105.4 8.2 %all_gather.24 = bf16[512,768]{1,0:T(8,128)(2,1)S(1)} all-gather(bf16[128,768]{1,0:T(8,128)(2,1)S(1)} %get-tuple-element.128), channel_id=1, replica_groups=mesh['dp'=8,'tensor'=4] {'tensor'}, dimensions={0}, use_global_device_ids=true | all-gather | bytes 983040 | tf_op jit(solution)/shard_map/all_gather | solution.py:44
  116.2 1.7 convolution_convert_fusion.2
  118.0 23.7 %reduce-scatter.11.cloned.1.call-done = bf16[128,768]{1,0:T(8,128)(2,1)} async-done(((bf16[512,768]{1,0:T(8,128)(2,1)}), bf16[128,768]{1,0:T(8,128)(2,1)}) %reduce-scatter.11.cloned.1.call-update) | async-done | bytes 196624 | tf_op jit(solution)/shard_map/reduce_scatter | solution.py:38
  144.2 8.5 %all_gather.25 = bf16[512,768]{1,0:T(8,128)(2,1)S(1)} all-gather(bf16[128,768]{1,0:T(8,128)(2,1)S(1)} %convert_element_type.108), channel_id=1, replica_groups=mesh['dp'=8,'tensor'=4] {'tensor'}, dimensions={0}, use_global_device_ids=true | all-gather | bytes 983040 | tf_op jit(solution)/shard_map/all_gather | solution.py:44
  160.9 2.0 convolution_convert_fusion.1
  171.4 14.3 %reduce-scatter.13.cloned.1.call-done = bf16[192,528]{1,0:T(8,128)(2,1)} async-done(((bf16[768,528]{1,0:T(8,128)(2,1)}), bf16[192,528]{1,0:T(8,128)(2,1)}) %reduce-scatter.13.cloned.1.call-update) | async-done | bytes 202768
  187.2 111.3 %all-reduce.2.cloned.1.call-done = bf16[1536,768]{1,0:T(8,128)(2,1)} async-done(((bf16[1536,768]{1,0:T(8,128)(2,1)}), bf16[1536,768]{1,0:T(8,128)(2,1)}) %all-reduce.2.cloned.1.call-update) | async-done | bytes 2359312 | tf_op jit(solution)/shard_map/psum | solution.py:166
  298.5 1.9 copy.106
  300.6 8.0 %all_to_all.19 = bf16[128,4,192]{0,2,1:T(8,128)(2,1)S(1)} all-to-all(bf16[128,4,192]{0,2,1:T(8,128)(2,1)S(1)} %bitcast.97), channel_id=1, replica_groups=mesh['dp'=8,'tensor'=4] {'tensor'}, dimensions={1} | all-to-all | bytes 393216 | tf_op jit(solution)/shard_map/all_to_all | solution.py:153
  310.4 2.5 slice_convert_fusion
  312.9 130.6 %all-gather.8.cloned.1.call-done = bf16[8,3084,192]{1,2,0:T(8,128)(2,1)} async-done(((bf16[1,3084,192]{1,2,0:T(8,128)(2,1)}), bf16[8,3084,192]{1,2,0:T(8,128)(2,1)}) %all-gather.8.cloned.1.call-update) | async-done | bytes 9474064 | tf_op jit(solution)/shard_map/all_gather | solution.py:237
  443.5 5.8 %reduce_sum.192 = bf16[3084,192]{0,1:T(8,128)(2,1)S(1)} reduce(bf16[8,3084,192]{1,2,0:T(8,128)(2,1)} %all-gather.8.cloned.1.call-done, bf16[]{:T(256)} %constant.45.clone.1), dimensions={0}, to_apply=%region_24.25 | reduce | flops 4144896 | bytes 10658306 | tf_op jit(solution)/shard_map/reduce_sum | solution.py:238
  455.2 1.9 copy.107
  457.2 2.6 reshape.177
  459.8 4.2 copy.111
  464.0 2.4 slice_reduce_fusion
  (173 shorter events, 47.7 us)
Async XLA Ops:
  7.2 67.3 %copy-start = (bf16[768,768]{1,0:T(8,128)(2,1)S(1)}, bf16[768,768]{1,0:T(8,128)(2,1)}, u32[]{:S(2)}) copy-start(bf16[768,768]{1,0:T(8,128)(2,1)} %param.23) | copy-start | bytes 3538948
  7.2 25.4 %all-gather.6.cloned.1.call-start = ((), (), s32[]{:S(2)}) async-start(), calls=%async_computation.5 | async-start | bytes 1966080 | tf_op jit(solution)/shard_map/all_gather | solution.py:97
  9.2 53.8 %reduce-scatter.7.cloned.1.call-start = ((), (), s32[]{:S(2)}) async-start(), calls=%async_computation.6 | async-start | bytes 983040 | tf_op jit(solution)/shard_map/reduce_scatter | solution.py:38
  39.5 63.3 %reduce-scatter.9.cloned.1.call-start = ((), (), s32[]{:S(2)}) async-start(), calls=%async_computation.7 | async-start | bytes 983040 | tf_op jit(solution)/shard_map/reduce_scatter | solution.py:38
  46.2 28.2 %copy-start.32 = (f32[768]{0:T(1024)S(1)}, f32[768]{0:T(1024)}, u32[]{:S(2)}) copy-start(f32[768]{0:T(1024)} %param.24) | copy-start | bytes 9220
  74.5 2.0 copy-start.9
  74.5 2.9 copy-start.30
  77.4 25.5 %copy-start.4 = (bf16[128,768]{1,0:T(8,128)(2,1)S(1)}, bf16[128,768]{1,0:T(8,128)(2,1)}, u32[]{:S(2)}) copy-start(bf16[128,768]{1,0:T(8,128)(2,1)} %reduce-scatter.7.cloned.1.call-done) | copy-start | bytes 589828
  79.1 62.7 %reduce-scatter.11.cloned.1.call-start = ((), (), s32[]{:S(2)}) async-start(), calls=%async_computation.8 | async-start | bytes 983040 | tf_op jit(solution)/shard_map/reduce_scatter | solution.py:38
  104.3 9.4 %copy-start.31 = (bf16[768,768]{1,0:T(8,128)(2,1)S(1)}, bf16[768,768]{1,0:T(8,128)(2,1)}, u32[]{:S(2)}) copy-start(bf16[768,768]{1,0:T(8,128)(2,1)} %param.25) | copy-start | bytes 3538948
  104.3 9.4 %copy-start.36 = (f32[512,768]{1,0:T(8,128)S(1)}, f32[512,768]{1,0:T(8,128)}, u32[]{:S(2)}) copy-start(f32[512,768]{1,0:T(8,128)} %get-tuple-element.145) | copy-start | bytes 4718596
  117.9 67.8 %reduce-scatter.13.cloned.1.call-start = ((), (), s32[]{:S(2)}) async-start(), calls=%async_computation.11 | async-start | bytes 1228800
  144.2 9.1 %copy-start.3 = (f32[3,512,512]{1,2,0:T(8,128)S(1)}, f32[3,512,512]{1,2,0:T(8,128)}, u32[]{:S(2)}) copy-start(f32[3,512,512]{1,2,0:T(8,128)} %copy-done.2) | copy-start | bytes 9437188
  144.2 9.1 %copy-start.19 = (f32[3,512]{1,0:T(4,128)S(1)}, f32[3,512]{1,0:T(4,128)}, u32[]{:S(2)}) copy-start(f32[3,512]{1,0:T(4,128)} %copy-done.18) | copy-start | bytes 18436
  154.9 3.1 copy-start.17
  160.8 2.1 copy-start.10
  160.8 137.7 %all-reduce.2.cloned.1.call-start = ((), (), s32[]{:S(2)}) async-start(), calls=%async_computation.9 | async-start | bytes 4718592 | tf_op jit(solution)/shard_map/psum | solution.py:166
  160.9 2.1 copy-start.35
  165.4 278.1 %all-gather.8.cloned.1.call-start = ((), (), s32[]{:S(2)}) async-start(), calls=%async_computation.10 | async-start | bytes 11059200 | tf_op jit(solution)/shard_map/all_gather | solution.py:237
  166.1 2.5 copy-start.5
  170.4 16.3 %copy-start.21 = (bf16[1,192]{1,0:T(2,128)(2,1)S(1)}, bf16[1,192]{1,0:T(2,128)(2,1)}, u32[]{:S(2)}) copy-start(bf16[1,192]{1,0:T(2,128)(2,1)} %reshape.176) | copy-start | bytes 1156
  300.4 8.9 %copy-start.16 = (bf16[192,528]{1,0:T(8,128)(2,1)S(1)}, bf16[192,528]{1,0:T(8,128)(2,1)}, u32[]{:S(2)}) copy-start(bf16[192,528]{1,0:T(8,128)(2,1)} %reduce-scatter.13.cloned.1.call-done) | copy-start | bytes 608260
  300.4 9.9 %copy-start.6 = (bf16[1536,768]{1,0:T(8,128)(2,1)S(1)}, bf16[1536,768]{1,0:T(8,128)(2,1)}, u32[]{:S(2)}) copy-start(bf16[1536,768]{1,0:T(8,128)(2,1)} %all-reduce.2.cloned.1.call-done) | copy-start | bytes 7077892
  457.2 9.2 %copy-start.1 = (bf16[768,768]{1,0:T(8,128)(2,1)S(1)}, bf16[768,768]{1,0:T(8,128)(2,1)}, u32[]{:S(2)}) copy-start(bf16[768,768]{1,0:T(8,128)(2,1)} %param.23) | copy-start | bytes 3538948
  (20 other events, 28.8 us)
Sparse Core Ops, SparseCore 0:
  10.2 22.3 all-gather.5
  39.7 23.2 reduce-scatter.6
  79.2 23.6 reduce-scatter.8
  118.0 23.6 reduce-scatter.10
  160.9 24.7 reduce-scatter.12
  189.8 108.7 all-reduce.1
  301.5 141.8 all-gather.7
